TPU v7x, 32 devices: a whole 2x2x4 slice. The times are simulated.
32 devices in a mesh: replica: 8 (over y, x, core), shard: 4 (over z).
Axes of the slice: x: 2, y: 2, z: 4, core: 2. Of those that a mesh axis runs over, the one named last changes fastest.
Arguments:
- tokens: bfloat16 [32768, 768], P(('replica', 'shard')), may hold values from -6 to 6
- cotangent: bfloat16 [32768, 768], P(('replica', 'shard')), may hold values from -6 to 6
- segments: int32 [32, 1024], P(('replica', 'shard')), may hold values from 0 to 3, never falling along the last dimension, each value on 1 to 512 neighbouring positions
- routes: int32 [32768, 1], P(('replica', 'shard')), may hold values from 0 to 3; in each aligned block of 1024 rows (0 to 1023, 1024 to 2047, ...) at most 320 rows name the same one
- w_query: bfloat16 [768, 768], P('shard'), may hold values from -0.02734375 to 0.02734375
- w_key: bfloat16 [768, 768], P('shard'), may hold values from -0.21875 to 0.21875
- w_value: bfloat16 [768, 768], P('shard'), may hold values from -0.21875 to 0.21875
- w_output: bfloat16 [768, 768], P('shard'), may hold values from -1.75 to 1.75
- norm_attn: bfloat16 [768], P('shard'), may hold values from 0.5 to 1.5
- norm_ffn: bfloat16 [768], P('shard'), may hold values from 0.5 to 1.5
- w_router: bfloat16 [768, 4], P('shard'), may hold values from -0.15625 to 0.15625
- rel_bias: bfloat16 [32, 12], P('shard'), may hold values from -4 to 4
- expert_input_weight: bfloat16 [4, 768, 3072], P('shard'), may hold values from -0.21875 to 0.21875
- expert_output_weight: bfloat16 [4, 3072, 768], P('shard'), may hold values from -0.4375 to 0.4375
Outputs:
- mixed: bfloat16 [32768, 768], P(('replica', 'shard'))
- grad_tokens: float32 [32768, 768], P(('replica', 'shard'))
- grad_query: float32 [768, 768], P('shard')
- grad_key: float32 [768, 768], P('shard')
- grad_value: float32 [768, 768], P('shard')
- grad_output: float32 [768, 768], P('shard')
- grad_norm_attn: float32 [768], P('shard')
- grad_norm_ffn: float32 [768], P('shard')
- grad_router: float32 [768, 4], P('shard')
- grad_rel_bias: float32 [32, 12], P('shard')
- grad_expert_in: float32 [4, 768, 3072], P('shard')
- grad_expert_out: float32 [4, 3072, 768], P('shard')
Inputs may be any that keep to these rules, and one draw needn't show every extreme that they name: `segments`: within a sequence the segment numbers never fall; each of the 4 numbers covers 1 to 512 positions, and one covers exactly 512. `routes`: among the 1024 rows of one device no expert is named more than 320 times, and in some device's rows an expert is named exactly 320 times; every expert is named somewhere.
All inputs are finite; a program needn't handle non-finite values.
Results may differ from a plain program's by a relative error of at most 0.014.
Values may be sent and summed in bfloat16 or wider, within the bound.
No kernel may reach another device: no remote copies, remote signals or barrier semaphores. Data moves between devices by JAX's collectives and lax.ppermute only.
A program may use at most 320 MiB of HBM per device.

v0:
```python
from functools import partial
import jax
import jax.numpy as jnp
from jax import lax
from jax.sharding import PartitionSpec as P

highest = lax.Precision.HIGHEST
far_steps = (12, 16, 23, 32, 46, 64, 91)


def bucket_table(query_pos, key_pos):
    relative = key_pos[None, :] - query_pos[:, None]
    distance = jnp.abs(relative)
    beyond = jnp.zeros_like(distance)
    for threshold in far_steps:
        beyond = beyond + (distance >= threshold).astype(jnp.int32)
    inside = jnp.where(distance < 8, distance, 8 + beyond)
    return inside + 16 * (relative > 0).astype(jnp.int32)


def rms_norm(values_in, gain_vec):
    return (
        values_in
        * lax.rsqrt(jnp.mean(values_in * values_in, axis=-1, keepdims=True) + 1e-06)
        * gain_vec
    )


def block_scores(queries, key_rows, relative_bias_table, slot_indicators, allowed):
    raw_dot = jnp.einsum("qhe,khe->hqk", queries, key_rows, preferred_element_type=jnp.float32)
    relative_bias_term = jnp.einsum(
        "rni,rf->fni", slot_indicators, relative_bias_table, preferred_element_type=jnp.float32
    )
    scores = raw_dot + relative_bias_term
    return jnp.where(allowed[None], scores, -1e30)


def expert_forward(rows_in, first_all, second_all):
    before_activation = jnp.einsum(
        "ecd,edf->ecf", rows_in, first_all, preferred_element_type=jnp.float32
    )
    hidden = jax.nn.gelu(before_activation).astype(jnp.bfloat16)
    result = jnp.einsum(
        "ecf,efd->ecd", hidden, second_all, preferred_element_type=jnp.float32
    ).astype(jnp.bfloat16)
    return (before_activation, hidden, result)


def expert_backward(rows_in, before_activation, hidden, grad_result, first_all, second_all):
    grad_hidden = jnp.einsum(
        "ecd,efd->ecf", grad_result, second_all, preferred_element_type=jnp.float32
    )
    grad_second = jnp.einsum(
        "ecf,ecd->efd", hidden, grad_result, preferred_element_type=jnp.float32
    )
    grad_pre = jax.vjp(jax.nn.gelu, before_activation)[1](grad_hidden)[0].astype(jnp.bfloat16)
    grad_first = jnp.einsum("ecd,ecf->edf", rows_in, grad_pre, preferred_element_type=jnp.float32)
    grad_rows = jnp.einsum(
        "ecf,edf->ecd", grad_pre, first_all, preferred_element_type=jnp.float32
    ).astype(jnp.bfloat16)
    return (grad_first, grad_second, grad_rows)


def on_device(
    tokens,
    cotangent,
    segments,
    routes,
    w_query,
    w_key,
    w_value,
    w_output,
    norm_attn,
    norm_ffn,
    w_router,
    rel_bias,
    expert_input_weight,
    expert_output_weight,
):
    gathered = (
        lax.all_gather(w_query, "shard", axis=0, tiled=True),
        lax.all_gather(w_key, "shard", axis=0, tiled=True),
        lax.all_gather(w_value, "shard", axis=0, tiled=True),
        lax.all_gather(w_output, "shard", axis=0, tiled=True),
        lax.all_gather(norm_attn, "shard", axis=0, tiled=True),
        lax.all_gather(norm_ffn, "shard", axis=0, tiled=True),
        lax.all_gather(w_router, "shard", axis=0, tiled=True),
        lax.all_gather(rel_bias, "shard", axis=0, tiled=True),
    )
    (
        full_query,
        full_key,
        full_value,
        full_output,
        gain_one,
        gain_two,
        router,
        relative_bias_table,
    ) = gathered
    seq_count, length = segments.shape
    row_count, model_width = tokens.shape
    bucket_count, head_count = relative_bias_table.shape
    head_width = model_width // head_count
    experts = router.shape[1]
    qblock = min(512, length)
    positions = jnp.arange(length, dtype=jnp.int32)
    labels = jnp.arange(bucket_count, dtype=jnp.int32)

    def block_frame(which, offset):
        query_pos = positions[offset : offset + qblock]
        matches = bucket_table(query_pos, positions)[None] == labels[:, None, None]
        segment_row = segments[which]
        allowed = segment_row[offset : offset + qblock][:, None] == segment_row[None, :]
        return (matches, allowed)

    inputs = tokens.astype(jnp.float32)
    gain_one_f = gain_one.astype(jnp.float32)
    normed_one = rms_norm(inputs, gain_one_f).astype(jnp.bfloat16)

    def project(weight_mat):
        product = jnp.dot(normed_one, weight_mat, preferred_element_type=jnp.float32)
        return product.astype(jnp.bfloat16).reshape(seq_count, length, head_count, head_width)

    queries = project(full_query)
    key_rows = project(full_key)
    value_rows = project(full_value)
    pieces = []
    log_sums = []
    which = 0
    for offset in range(0, length, qblock):
        matches, allowed = block_frame(which, offset)
        scores = block_scores(
            queries[which, offset : offset + qblock],
            key_rows[which],
            relative_bias_table,
            matches.astype(jnp.bfloat16),
            allowed,
        )
        highest_score = jnp.max(scores, axis=-1, keepdims=True)
        shifted = jnp.exp(scores - highest_score)
        denominator = jnp.sum(shifted, axis=-1, keepdims=True)
        chances = (shifted / denominator).astype(jnp.bfloat16)
        log_sums.append(highest_score + jnp.log(denominator))
        pieces.append(
            jnp.einsum(
                "hqk,khe->qhe", chances, value_rows[which], preferred_element_type=jnp.float32
            )
        )
    attended = jnp.concatenate(pieces, 0).reshape(row_count, model_width).astype(jnp.bfloat16)
    branch = jnp.dot(attended, full_output, preferred_element_type=jnp.float32)
    middle = inputs + branch
    gain_two_f = gain_two.astype(jnp.float32)
    normed_two = rms_norm(middle, gain_two_f).astype(jnp.bfloat16)
    normed_two_f = normed_two.astype(jnp.float32)
    router_f = router.astype(jnp.float32)
    logits = jnp.dot(normed_two_f, router_f, precision=highest)
    gate_probs = jax.nn.softmax(logits, axis=-1)
    chosen = (routes == jnp.arange(experts, dtype=jnp.int32)[None, :]).astype(jnp.int32)
    chosen_f = chosen.astype(jnp.float32)
    chosen_gate = jnp.sum(gate_probs * chosen_f, axis=-1)
    slot_index = jnp.cumsum(chosen, axis=0) - chosen
    capacity = 5 * row_count // (4 * experts)
    slot_range = jnp.arange(capacity, dtype=jnp.int32)
    places = (
        (chosen.T[:, None, :] == 1) & (slot_index.T[:, None, :] == slot_range[None, :, None])
    ).astype(jnp.bfloat16)
    outgoing = jnp.einsum(
        "ect,td->ecd", places, normed_two, preferred_element_type=jnp.float32
    ).astype(jnp.bfloat16)
    arrived = lax.all_to_all(outgoing, "shard", split_axis=0, concat_axis=1, tiled=True)
    before_activation, hidden, result = expert_forward(
        arrived, expert_input_weight, expert_output_weight
    )
    returned = lax.all_to_all(result, "shard", split_axis=1, concat_axis=0, tiled=True)
    combined = jnp.einsum("ect,ecd->td", places, returned, preferred_element_type=jnp.float32)
    mixed_out = (middle + chosen_gate[:, None] * combined).astype(jnp.bfloat16)
    again = (
        lax.all_gather(w_query, "shard", axis=0, tiled=True),
        lax.all_gather(w_key, "shard", axis=0, tiled=True),
        lax.all_gather(w_value, "shard", axis=0, tiled=True),
        lax.all_gather(w_output, "shard", axis=0, tiled=True),
        lax.all_gather(norm_attn, "shard", axis=0, tiled=True),
        lax.all_gather(norm_ffn, "shard", axis=0, tiled=True),
        lax.all_gather(w_router, "shard", axis=0, tiled=True),
        lax.all_gather(rel_bias, "shard", axis=0, tiled=True),
    )
    (
        full_query,
        full_key,
        full_value,
        full_output,
        gain_one,
        gain_two,
        router,
        relative_bias_table,
    ) = again
    gain_one_f = gain_one.astype(jnp.float32)
    gain_two_f = gain_two.astype(jnp.float32)
    router_f = router.astype(jnp.float32)
    grad_final = cotangent.astype(jnp.float32)
    grad_gate = jnp.sum(grad_final * combined, axis=-1)
    scaled = (chosen_gate[:, None] * grad_final).astype(jnp.bfloat16)
    grad_slots = jnp.einsum(
        "ect,td->ecd", places, scaled, preferred_element_type=jnp.float32
    ).astype(jnp.bfloat16)
    grad_arrived = lax.all_to_all(grad_slots, "shard", split_axis=0, concat_axis=1, tiled=True)
    grad_first, grad_second, grad_rows = expert_backward(
        arrived, before_activation, hidden, grad_arrived, expert_input_weight, expert_output_weight
    )
    grad_back = lax.all_to_all(grad_rows, "shard", split_axis=1, concat_axis=0, tiled=True)
    grad_normed_two = jnp.einsum(
        "ect,ecd->td", places, grad_back, preferred_element_type=jnp.float32
    )
    grad_probs_gate = chosen_f * grad_gate[:, None]
    grad_logits = jax.vjp(partial(jax.nn.softmax, axis=-1), logits)[1](grad_probs_gate)[0]
    grad_router = jnp.dot(normed_two_f.T, grad_logits, precision=highest)
    grad_normed_two = grad_normed_two + jnp.dot(grad_logits, router_f.T, precision=highest)
    pull_two = jax.vjp(rms_norm, middle, gain_two_f)[1]
    grad_mid_norm, grad_gain_two = pull_two(grad_normed_two)
    grad_middle = grad_final + grad_mid_norm
    gradient_residual_branch = grad_middle.astype(jnp.bfloat16)
    grad_wout = jnp.einsum(
        "td,te->de", attended, gradient_residual_branch, preferred_element_type=jnp.float32
    )
    grad_attended = jnp.einsum(
        "te,de->td", gradient_residual_branch, full_output, preferred_element_type=jnp.float32
    )
    grad_attended = grad_attended.astype(jnp.bfloat16).reshape(
        seq_count, length, head_count, head_width
    )
    query_grads = []
    grad_table = jnp.zeros((bucket_count, head_count), jnp.float32)
    block_index = 0
    which = 0
    key_acc = jnp.zeros((length, head_count, head_width), jnp.float32)
    value_acc = jnp.zeros((length, head_count, head_width), jnp.float32)
    for offset in range(0, length, qblock):
        matches, allowed = block_frame(which, offset)
        query_part = queries[which, offset : offset + qblock]
        scores = block_scores(
            query_part, key_rows[which], relative_bias_table, matches.astype(jnp.bfloat16), allowed
        )
        chances = jnp.exp(scores - log_sums[block_index])
        grad_part = grad_attended[which, offset : offset + qblock]
        value_acc = value_acc + jnp.einsum(
            "hqk,qhe->khe",
            chances.astype(jnp.bfloat16),
            grad_part,
            preferred_element_type=jnp.float32,
        )
        grad_chances = jnp.einsum(
            "qhe,khe->hqk", grad_part, value_rows[which], preferred_element_type=jnp.float32
        )
        inner_sum = jnp.sum(chances * grad_chances, axis=-1, keepdims=True)
        grad_scores = chances * (grad_chances - inner_sum)
        grad_table = grad_table + jnp.einsum(
            "vsi,dsi->dv",
            grad_scores,
            matches.astype(jnp.float32),
            precision=highest,
            preferred_element_type=jnp.float32,
        )
        grad_raw = grad_scores.astype(jnp.bfloat16)
        query_grads.append(
            jnp.einsum(
                "hqk,khe->qhe", grad_raw, key_rows[which], preferred_element_type=jnp.float32
            )
        )
        key_acc = key_acc + jnp.einsum(
            "hqk,qhe->khe", grad_raw, query_part, preferred_element_type=jnp.float32
        )
        block_index = block_index + 1
    key_grads = [key_acc]
    value_grads = [value_acc]
    grad_q = jnp.concatenate(query_grads, 0).reshape(row_count, model_width).astype(jnp.bfloat16)
    grad_k = jnp.stack(key_grads).reshape(row_count, model_width).astype(jnp.bfloat16)
    grad_v = jnp.stack(value_grads).reshape(row_count, model_width).astype(jnp.bfloat16)
    grad_wq = jnp.einsum("td,te->de", normed_one, grad_q, preferred_element_type=jnp.float32)
    grad_wk = jnp.einsum("td,te->de", normed_one, grad_k, preferred_element_type=jnp.float32)
    grad_wv = jnp.einsum("td,te->de", normed_one, grad_v, preferred_element_type=jnp.float32)
    grad_normed_one = jnp.einsum(
        "te,de->td", grad_q, full_query, preferred_element_type=jnp.float32
    )
    grad_normed_one = grad_normed_one + jnp.einsum(
        "te,de->td", grad_k, full_key, preferred_element_type=jnp.float32
    )
    grad_normed_one = grad_normed_one + jnp.einsum(
        "te,de->td", grad_v, full_value, preferred_element_type=jnp.float32
    )
    pull_one = jax.vjp(rms_norm, inputs, gain_one_f)[1]
    grad_in_norm, grad_gain_one = pull_one(grad_normed_one)
    grad_inputs = grad_middle + grad_in_norm
    owned_grads = (
        lax.psum_scatter(grad_wq, "shard", scatter_dimension=0, tiled=True),
        lax.psum_scatter(grad_wk, "shard", scatter_dimension=0, tiled=True),
        lax.psum_scatter(grad_wv, "shard", scatter_dimension=0, tiled=True),
        lax.psum_scatter(grad_wout, "shard", scatter_dimension=0, tiled=True),
        lax.psum_scatter(grad_gain_one, "shard", scatter_dimension=0, tiled=True),
        lax.psum_scatter(grad_gain_two, "shard", scatter_dimension=0, tiled=True),
        lax.psum_scatter(grad_router, "shard", scatter_dimension=0, tiled=True),
        lax.psum_scatter(grad_table, "shard", scatter_dimension=0, tiled=True),
    )
    summed_grads = lax.psum(
        (
            owned_grads[0],
            owned_grads[1],
            owned_grads[2],
            owned_grads[3],
            owned_grads[4],
            owned_grads[5],
            owned_grads[6],
            owned_grads[7],
        ),
        "replica",
    )
    replica_parts = (
        lax.psum_scatter(grad_first, "replica", scatter_dimension=2, tiled=True),
        lax.psum_scatter(grad_second, "replica", scatter_dimension=1, tiled=True),
    )
    total_first, total_second = (
        lax.all_gather(replica_parts[0], "replica", axis=2, tiled=True),
        lax.all_gather(replica_parts[1], "replica", axis=1, tiled=True),
    )
    return (
        mixed_out,
        grad_inputs,
        summed_grads[0],
        summed_grads[1],
        summed_grads[2],
        summed_grads[3],
        summed_grads[4],
        summed_grads[5],
        summed_grads[6],
        summed_grads[7],
        total_first,
        total_second,
    )


def solution(mesh):
    placed = (
        P(("replica", "shard"), None),
        P(("replica", "shard"), None),
        P(("replica", "shard"), None),
        P(("replica", "shard"), None),
        P("shard", None),
        P("shard", None),
        P("shard", None),
        P("shard", None),
        P("shard"),
        P("shard"),
        P("shard", None),
        P("shard", None),
        P("shard", None, None),
        P("shard", None, None),
    )
    return jax.shard_map(
        on_device,
        mesh=mesh,
        in_specs=placed,
        out_specs=(
            P(("replica", "shard"), None),
            P(("replica", "shard"), None),
            P("shard", None),
            P("shard", None),
            P("shard", None),
            P("shard", None),
            P("shard"),
            P("shard"),
            P("shard", None),
            P("shard", None),
            P("shard", None, None),
            P("shard", None, None),
        ),
        check_vma=False,
    )
```

profile of v0, /device:TPU:0, one launch (start us, length us, event | category | flops | bytes accessed | tf_op | source)
XLA Modules:
  0.0 1068.2 jit_solution(8149581946401056184)
XLA Ops:
  13.6 13.6 %all-reduce.8 = (bf16[768]{0:T(1024)(128)(2,1)S(1)}, bf16[768]{0:T(1024)(128)(2,1)S(1)}) all-reduce(bf16[768]{0:T(1024)(128)(2,1)S(1)} %dynamic-update-slice, bf16[768]{0:T(1024)(128)(2,1)S(1)} %dynamic-update-slice.1), channel_id=1, replica_groups=mesh['replica'=8,'shard'=4] {'shard'}, use_global_device_ids=true, to_apply=%add | all-reduce | flops 1536 | bytes 6144
  29.9 12.1 %all_gather.42 = bf16[32,12]{1,0:T(8,128)(2,1)S(1)} all-gather(bf16[8,12]{1,0:T(8,128)(2,1)} %param.25), channel_id=1, replica_groups=mesh['replica'=8,'shard'=4] {'shard'}, dimensions={0}, use_global_device_ids=true | all-gather | bytes 960 | tf_op jit(solution)/shard_map/all_gather | solution.py:88
  54.6 16.3 %fusion.1 = f32[512,1024,12]{0,2,1:T(8,128)} fusion(s32[512,1024]{0,1:T(8,128)S(1)} %fusion.85, bf16[32,12]{1,0:T(8,128)(2,1)S(1)} %all_gather.42), kind=kOutput, calls=%fused_computation.2 | convolution fusion | flops 419430400 | bytes 27263744 | tf_op jit(solution)/shard_map/rni,rf->fni/dot_general | solution.py:31
  70.9 29.9 %copy.81 = f32[512,1024,12]{1,0,2:T(8,128)} copy(f32[512,1024,12]{0,2,1:T(8,128)} %fusion.1) | data formatting | bytes 50331648 | tf_op jit(solution)/shard_map/rni,rf->fni/dot_general | solution.py:31
  100.9 16.5 %fusion.3 = f32[512,1024,12]{0,2,1:T(8,128)} fusion(s32[512,1024]{0,1:T(8,128)S(1)} %fusion.84, bf16[32,12]{1,0:T(8,128)(2,1)S(1)} %all_gather.42), kind=kOutput, calls=%fused_computation.5 | convolution fusion | flops 419430400 | bytes 27263744 | tf_op jit(solution)/shard_map/rni,rf->fni/dot_general | solution.py:31
  117.4 30.6 %copy.80 = f32[512,1024,12]{1,0,2:T(8,128)} copy(f32[512,1024,12]{0,2,1:T(8,128)} %fusion.3) | data formatting | bytes 50331648 | tf_op jit(solution)/shard_map/rni,rf->fni/dot_general | solution.py:31
  156.3 16.6 %fusion.161 = (f32[12,512]{1,0:T(8,128)S(1)}, f32[12,512,1024]{2,1,0:T(8,128)}) fusion(f32[512,1024,12]{1,0,2:T(8,128)} %copy.81, bf16[1024,12,64]{0,2,1:T(8,128)(2,1)S(1)} %bitcast.170, bf16[1,1024,12,64]{1,3,2,0:T(8,128)(2,1)} %bitcast.190, pred[512,1024]{1,0:T(8,128)(4,1)} %get-tuple-element.82), kind=kOutput, calls=%fused_computation.199 | convolution fusion | flops 824174592 | bytes 53239808 | tf_op jit(solution)/shard_map/qhe,khe->hqk/dot_general | solution.py:30
  172.9 11.4 %fusion.11 = f32[12,512]{1,0:T(8,128)S(1)} fusion(f32[12,512,1024]{2,1,0:T(8,128)} %get-tuple-element.88, f32[12,512]{1,0:T(8,128)S(1)} %get-tuple-element.87), kind=kLoop, calls=%fused_computation.27 | loop fusion | flops 12576768 | bytes 25214976 | tf_op jit(solution)/shard_map/reduce_sum | solution.py:141
  187.2 12.0 %fusion.133 = bf16[512,12,64]{0,2,1:T(8,128)(2,1)} fusion(bf16[1024,12,64]{0,2,1:T(8,128)(2,1)S(1)} %bitcast.180, f32[12,512,1024]{2,1,0:T(8,128)} %get-tuple-element.88, f32[12,512]{1,0:T(8,128)S(1)} %fusion.11, f32[12,512]{1,0:T(8,128)S(1)} %get-tuple-element.87), kind=kOutput, calls=%fused_computation.151 | convolution fusion | flops 824573952 | bytes 27574272 | tf_op jit(solution)/shard_map/hqk,khe->qhe/dot_general | solution.py:145
  199.1 15.7 %fusion.162 = (f32[12,512]{1,0:T(8,128)S(1)}, f32[12,512,1024]{2,1,0:T(8,128)}) fusion(f32[512,1024,12]{1,0,2:T(8,128)} %copy.80, bf16[1024,12,64]{0,2,1:T(8,128)(2,1)S(1)} %bitcast.171, bf16[1,1024,12,64]{1,3,2,0:T(8,128)(2,1)S(1)} %bitcast.191, pred[512,1024]{1,0:T(8,128)(4,1)} %get-tuple-element.81), kind=kOutput, calls=%fused_computation.200 | convolution fusion | flops 824174592 | bytes 53239808 | tf_op jit(solution)/shard_map/qhe,khe->hqk/dot_general | solution.py:30
  245.1 44.4 %all_to_all.42 = bf16[4,320,768]{2,1,0:T(8,128)(2,1)S(1)} all-to-all(bf16[4,320,768]{2,1,0:T(8,128)(2,1)S(1)} %fusion.104), channel_id=1, replica_groups=mesh['replica'=8,'shard'=4] {'shard'}, dimensions={0} | all-to-all | bytes 3932160 | tf_op jit(solution)/shard_map/all_to_all | solution.py:170
  306.9 15.1 %copy.116 = bf16[1,1280,768]{2,0,1:T(2,128)(2,1)} copy(bf16[1,1280,768]{2,1,0:T(8,128)(2,1)S(1)} %fusion.70) | data formatting | bytes 3932160 | tf_op jit(solution)/shard_map/convert_element_type | solution.py:45
  322.5 13.7 %reduce.2 = bf16[1280,768]{1,0:T(8,128)(2,1)} reduce(bf16[1280,1,768]{2,1,0:T(2,128)(2,1)} %bitcast.174, bf16[]{:T(256)} %broadcast.378), dimensions={1}, to_apply=%bitcast.168.reduce_sub_computation | reduce | bytes 3932162
  344.7 48.8 %all-gather = bf16[4,192,4]{1,2,0:T(4,128)(2,1)S(1)} all-gather(bf16[1,192,4]{1,2,0:T(4,128)(2,1)S(1)} %bitcast.216), channel_id=1, replica_groups=mesh['replica'=8,'shard'=4] {'shard'}, dimensions={0}, use_global_device_ids=true | all-gather | bytes 7680 | tf_op jit(solution)/shard_map/all_gather | solution.py:87
  412.3 44.4 %all_to_all.43 = bf16[4,320,768]{2,1,0:T(8,128)(2,1)S(1)} all-to-all(bf16[4,320,768]{2,1,0:T(8,128)(2,1)S(1)} %fusion.107), channel_id=1, replica_groups=mesh['replica'=8,'shard'=4] {'shard'}, dimensions={0} | all-to-all | bytes 3932160 | tf_op jit(solution)/shard_map/all_to_all | solution.py:206
  468.1 19.0 %fusion.20 = bf16[1280,3072]{1,0:T(8,128)(2,1)S(1)} fusion(f32[1280,3072]{1,0:T(8,128)} %copy-done.54, bf16[1280,768]{1,0:T(8,128)(2,1)} %bitcast.197, bf16[1,3072,768]{2,1,0:T(8,128)(2,1)} %param.27), kind=kOutput, calls=%fused_computation.36 | convolution fusion | flops 6118440960 | bytes 30277632 | tf_op jit(solution)/shard_map/ecd,efd->ecf/dot_general | solution.py:50
  509.5 15.3 %copy.115 = bf16[1,1280,768]{2,0,1:T(2,128)(2,1)} copy(bf16[1,1280,768]{2,1,0:T(8,128)(2,1)S(1)} %fusion.73) | data formatting | bytes 3932160 | tf_op jit(solution)/shard_map/convert_element_type | solution.py:60
  524.8 13.8 %reduce.3 = bf16[1280,768]{1,0:T(8,128)(2,1)} reduce(bf16[1280,1,768]{2,1,0:T(2,128)(2,1)} %bitcast.175, bf16[]{:T(256)} %broadcast.378), dimensions={1}, to_apply=%bitcast.167.reduce_sub_computation | reduce | bytes 3932162
  550.7 39.7 %all-to-all-done.3 = bf16[4,2,122880]{2,1,0:T(2,128)(2,1)} async-done(((bf16[4,2,122880]{2,1,0:T(2,128)(2,1)}), bf16[4,2,122880]{2,1,0:T(2,128)(2,1)}, u32[]{:S(2)}, u32[]{:S(2)}) %all-to-all-start.3) | async-done | bytes 1966112 | tf_op jit(solution)/shard_map/all_to_all | solution.py:210
  639.5 16.2 %multiply_reduce_fusion = (f32[12,512]{1,0:T(8,128)S(1)}, f32[12,512,1024]{2,1,0:T(8,128)}) fusion(f32[12,512,1024]{2,1,0:T(8,128)} %get-tuple-element.88, f32[12,512]{1,0:T(8,128)S(1)} %log_add_fusion, bf16[1024,12,64]{0,2,1:T(8,128)(2,1)S(1)} %bitcast.182, bf16[1,1024,12,64]{1,3,2,0:T(8,128)(2,1)} %bitcast.188), kind=kOutput, calls=%fused_computation.15 | convolution fusion | flops 824174592 | bytes 52740096 | tf_op jit(solution)/shard_map/qhe,khe->hqk/dot_general | solution.py:251
  655.7 16.0 %multiply_reduce_fusion.1 = (f32[12,512]{1,0:T(8,128)S(1)}, f32[12,512,1024]{2,1,0:T(8,128)}) fusion(f32[12,512,1024]{2,1,0:T(8,128)} %get-tuple-element.90, f32[12,512]{1,0:T(8,128)S(1)} %log_add_fusion.1, bf16[1024,12,64]{0,2,1:T(8,128)(2,1)S(1)} %bitcast.183, bf16[1,1024,12,64]{1,3,2,0:T(8,128)(2,1)} %bitcast.189), kind=kOutput, calls=%fused_computation.18 | convolution fusion | flops 824174592 | bytes 52740096 | tf_op jit(solution)/shard_map/qhe,khe->hqk/dot_general | solution.py:251
  671.8 26.1 %subtract_multiply_fusion = f32[12,512,1024]{2,1,0:T(8,128)} fusion(f32[12,512,1024]{2,1,0:T(8,128)} %get-tuple-element.99, f32[12,512,1024]{2,1,0:T(8,128)} %get-tuple-element.88, f32[12,512]{1,0:T(8,128)S(1)} %get-tuple-element.98, f32[12,512]{1,0:T(8,128)S(1)} %log_add_fusion), kind=kLoop, calls=%fused_computation.14 | loop fusion | flops 18874368 | bytes 75546624 | tf_op jit(solution)/shard_map/mul | solution.py:255
  697.9 13.4 %fusion.126 = bf16[512,12,64]{0,2,1:T(8,128)(2,1)} fusion(bf16[1024,12,64]{0,2,1:T(8,128)(2,1)S(1)} %bitcast.172, f32[12,512,1024]{2,1,0:T(8,128)} %subtract_multiply_fusion), kind=kOutput, calls=%fused_computation.148 | convolution fusion | flops 811991040 | bytes 27525120 | tf_op jit(solution)/shard_map/hqk,khe->qhe/dot_general | solution.py:265
  711.3 26.0 %subtract_multiply_fusion.1 = f32[12,512,1024]{2,1,0:T(8,128)} fusion(f32[12,512,1024]{2,1,0:T(8,128)} %get-tuple-element.101, f32[12,512,1024]{2,1,0:T(8,128)} %get-tuple-element.90, f32[12,512]{1,0:T(8,128)S(1)} %get-tuple-element.100, f32[12,512]{1,0:T(8,128)S(1)} %log_add_fusion.1), kind=kLoop, calls=%fused_computation.17 | loop fusion | flops 18874368 | bytes 75546624 | tf_op jit(solution)/shard_map/mul | solution.py:255
  737.3 13.1 %fusion.129 = bf16[512,12,64]{0,2,1:T(8,128)(2,1)} fusion(bf16[1024,12,64]{0,2,1:T(8,128)(2,1)S(1)} %bitcast.173, f32[12,512,1024]{2,1,0:T(8,128)} %subtract_multiply_fusion.1), kind=kOutput, calls=%fused_computation.149 | convolution fusion | flops 811991040 | bytes 27525120 | tf_op jit(solution)/shard_map/hqk,khe->qhe/dot_general | solution.py:265
  785.4 31.0 %copy.94 = f32[12,512,1024]{1,0,2:T(8,128)} copy(f32[12,512,1024]{2,1,0:T(8,128)} %subtract_multiply_fusion) | data formatting | bytes 50331648 | tf_op jit(solution)/shard_map/mul | solution.py:255
  816.4 31.0 %copy.93 = f32[12,512,1024]{1,0,2:T(8,128)} copy(f32[12,512,1024]{2,1,0:T(8,128)} %subtract_multiply_fusion.1) | data formatting | bytes 50331648 | tf_op jit(solution)/shard_map/mul | solution.py:255
  862.5 38.0 %fusion.134 = f32[32,12]{1,0:T(8,128)S(1)} fusion(f32[12,512,1024]{1,0,2:T(8,128)} %copy.93, s32[512,1024]{0,1:T(8,128)S(1)} %copy-done.3), kind=kOutput, calls=%fused_computation.152 | convolution fusion | flops 2432696320 | bytes 27264512 | tf_op jit(solution)/shard_map/vsi,dsi->dv/dot_general | solution.py:256
  902.0 39.7 %fusion.136 = f32[32,12]{1,0:T(8,128)S(1)} fusion(f32[32,12]{1,0:T(8,128)S(1)} %fusion.134, f32[12,512,1024]{1,0,2:T(8,128)} %copy.94, s32[512,1024]{0,1:T(8,128)S(1)} %copy-done.1), kind=kOutput, calls=%fused_computation.154 | convolution fusion | flops 2432696832 | bytes 27266048 | tf_op jit(solution)/shard_map/vsi,dsi->dv/dot_general | solution.py:256
  941.8 17.0 %all-reduce.7 = (f32[768]{0:T(1024)S(1)}, f32[768]{0:T(1024)S(1)}, f32[32,12]{1,0:T(8,128)S(1)}) all-reduce(f32[768]{0:T(1024)S(1)} %get-tuple-element.62, f32[768]{0:T(1024)S(1)} %copy-done.47, f32[32,12]{1,0:T(8,128)S(1)} %fusion.136), channel_id=6, replica_groups=mesh['replica'=8,'shard'=4] {'shard'}, use_global_device_ids=true, to_apply=%region_26.27.clone | all-reduce | flops 1920 | bytes 15360
  958.9 22.7 %all-reduce.5 = (f32[192]{0:T(256)}, f32[192]{0:T(256)}, f32[192,4]{0,1:T(4,128)}, f32[8,12]{1,0:T(8,128)}) all-reduce(f32[192]{0:T(256)S(1)} %dynamic-slice.3, f32[192]{0:T(256)S(1)} %dynamic-slice.5, f32[192,4]{0,1:T(4,128)S(1)} %copy.108, ...), channel_id=1, replica_groups=mesh['replica'=8,'shard'=4] {'replica'}, use_global_device_ids=true, to_apply=%region_27.28 | all-reduce | flops 1248 | bytes 9984 | tf_op jit(solution)/shard_map/psum | solution.py:303
  981.6 60.0 %all-reduce.11.cloned.1.call-done = (f32[192,768]{1,0:T(8,128)}, f32[192,768]{1,0:T(8,128)}, f32[192,768]{1,0:T(8,128)}, f32[192,768]{1,0:T(8,128)}) async-done(((f32[192,768]{1,0:T(8,128)}, f32[192,768]{1,0:T(8,128)}, f32[192,768]{1,0:T(8,128)}, f32[192,768]{1,0:T(8,128)}), (f32[192,768]{1,0:T(8,128)}, f32[192,768]{1,0:T(8,128)}, f32[192,768]{1,0:T(8,128)}, ...) | async-done | bytes 2359312 | tf_op jit(solution)/shard_map/psum | solution.py:303
  (271 shorter events, 272.0 us)
Async XLA Ops:
  7.2 142.4 %all-gather.10.cloned.1.call-start = ((), (), s32[]{:S(2)}) async-start(), calls=%async_computation.12 | async-start | bytes 1474560 | tf_op jit(solution)/shard_map/all_gather | solution.py:81
  7.9 145.6 %all-gather.12.cloned.1.call-start = ((), (), s32[]{:S(2)}) async-start(), calls=%async_computation.13 | async-start | bytes 1474560 | tf_op jit(solution)/shard_map/all_gather | solution.py:82
  8.7 175.6 %all-gather.8.cloned.1.call-start = ((), (), s32[]{:S(2)}) async-start(), calls=%async_computation.11 | async-start | bytes 1474560 | tf_op jit(solution)/shard_map/all_gather | solution.py:83
  9.4 228.3 %all-gather.14.cloned.1.call-start = ((), (), s32[]{:S(2)}) async-start(), calls=%async_computation.14 | async-start | bytes 1474560 | tf_op jit(solution)/shard_map/all_gather | solution.py:84
  27.3 157.0 %copy-start.40 = (f32[768]{0:T(1024)}, f32[768]{0:T(1024)S(1)}, u32[]{:S(2)}) copy-start(f32[768]{0:T(1024)S(1)} %convert_element_type.284) | copy-start | bytes 9220
  49.1 135.2 %copy-start.42 = (f32[1024]{0:T(1024)}, f32[1024]{0:T(1024)S(1)}, u32[]{:S(2)}) copy-start(f32[1024]{0:T(1024)S(1)} %fusion.146) | copy-start | bytes 12292
  51.2 49.7 %copy-start.2 = (s32[512,1024]{0,1:T(8,128)}, s32[512,1024]{0,1:T(8,128)S(1)}, u32[]{:S(2)}) copy-start(s32[512,1024]{0,1:T(8,128)S(1)} %fusion.84) | copy-start | bytes 6291460
  117.4 30.6 %copy-start.46 = (s32[1,1024]{1,0:T(1,128)S(1)}, s32[1,1024]{1,0:T(1,128)}, u32[]{:S(2)}) copy-start(s32[1,1024]{1,0:T(1,128)} %param.16) | copy-start | bytes 12292
  117.4 32.2 %copy-start.7 = (bf16[1024,768]{0,1:T(8,128)(2,1)S(1)}, bf16[1024,768]{0,1:T(8,128)(2,1)}, u32[]{:S(2)}) copy-start(bf16[1024,768]{0,1:T(8,128)(2,1)} %copy-done.6) | copy-start | bytes 4718596
  156.3 42.8 %copy-start.4 = (bf16[1024,768]{0,1:T(8,128)(2,1)}, bf16[1024,768]{0,1:T(8,128)(2,1)S(1)}, u32[]{:S(2)}) copy-start(bf16[1024,768]{0,1:T(8,128)(2,1)S(1)} %convolution_convert_fusion.1) | copy-start | bytes 4718596
  237.7 53.1 %slice-start.5 = ((s8[4718592]{0:T(1024)(128)(4,1)}), s8[4194304]{0:T(1024)(128)(4,1)S(1)}, s32[]{:S(2)}) async-start(s8[4718592]{0:T(1024)(128)(4,1)} %bitcast.219), calls=%async_computation.30 | async-start | bytes 8388608
  242.4 48.4 %slice-start.6 = ((s8[4718592]{0:T(1024)(128)(4,1)}), s8[524288]{0:T(1024)(128)(4,1)S(1)}, s32[]{:S(2)}) async-start(s8[4718592]{0:T(1024)(128)(4,1)} %bitcast.219), calls=%async_computation.31 | async-start | bytes 1048576
  242.4 54.9 %slice-start.3 = ((s8[4718592]{0:T(1024)(128)(4,1)}), s8[4194304]{0:T(1024)(128)(4,1)S(1)}, s32[]{:S(2)}) async-start(s8[4718592]{0:T(1024)(128)(4,1)} %bitcast.217), calls=%async_computation.28 | async-start | bytes 8388608
  340.2 58.0 %all-to-all-start.1 = ((bf16[4,2,122880]{2,1,0:T(2,128)(2,1)}), bf16[4,2,122880]{2,1,0:T(2,128)(2,1)}, u32[]{:S(2)}, u32[]{:S(2)}) async-start(bf16[4,2,122880]{2,1,0:T(2,128)(2,1)} %reshape.408), calls=%async_computation.1 | async-start | bytes 3932160 | tf_op jit(solution)/shard_map/all_to_all | solution.py:174
  344.6 437.1 %reduce-scatter.20.cloned.1.call-start = ((), (), s32[]{:S(2)}) async-start(), calls=%async_computation.21 | async-start | bytes 10616832 | tf_op jit(solution)/shard_map/reduce_scatter | solution.py:318
  405.5 52.5 %slice-start.7 = ((s8[15728640]{0:T(1024)(128)(4,1)}), s8[4194304]{0:T(1024)(128)(4,1)S(1)}, s32[]{:S(2)}) async-start(s8[15728640]{0:T(1024)(128)(4,1)} %bitcast.221), calls=%async_computation.32 | async-start | bytes 8388608
  405.5 52.5 %slice-start.8 = ((s8[15728640]{0:T(1024)(128)(4,1)}), s8[4194304]{0:T(1024)(128)(4,1)S(1)}, s32[]{:S(2)}) async-start(s8[15728640]{0:T(1024)(128)(4,1)} %bitcast.221), calls=%async_computation.33 | async-start | bytes 8388608
  409.6 48.4 %slice-start.9 = ((s8[15728640]{0:T(1024)(128)(4,1)}), s8[4194304]{0:T(1024)(128)(4,1)S(1)}, s32[]{:S(2)}) async-start(s8[15728640]{0:T(1024)(128)(4,1)} %bitcast.221), calls=%async_computation.34 | async-start | bytes 8388608
  409.6 48.4 %slice-start.10 = ((s8[15728640]{0:T(1024)(128)(4,1)}), s8[3145728]{0:T(1024)(128)(4,1)S(1)}, s32[]{:S(2)}) async-start(s8[15728640]{0:T(1024)(128)(4,1)} %bitcast.221), calls=%async_computation.35 | async-start | bytes 6291456
  468.1 314.2 %reduce-scatter.18.cloned.1.call-start = ((), (), s32[]{:S(2)}) async-start(), calls=%async_computation.19 | async-start | bytes 10616832 | tf_op jit(solution)/shard_map/reduce_scatter | solution.py:317
  542.5 47.9 %all-to-all-start.3 = ((bf16[4,2,122880]{2,1,0:T(2,128)(2,1)}), bf16[4,2,122880]{2,1,0:T(2,128)(2,1)}, u32[]{:S(2)}, u32[]{:S(2)}) async-start(bf16[4,2,122880]{2,1,0:T(2,128)(2,1)} %reshape.410), calls=%async_computation.3 | async-start | bytes 3932160 | tf_op jit(solution)/shard_map/all_to_all | solution.py:210
  546.9 237.4 %reduce-scatter.22.cloned.1.call-start = ((), (), s32[]{:S(2)}) async-start(), calls=%async_computation.23 | async-start | bytes 491520
  550.6 349.8 %reduce-scatter.16.cloned.1.call-start = ((), (), s32[]{:S(2)}) async-start(), calls=%async_computation.18 | async-start | bytes 2949120 | tf_op jit(solution)/shard_map/reduce_scatter | solution.py:297
  610.2 290.2 %reduce-scatter.14.cloned.1.call-start = ((), (), s32[]{:S(2)}) async-start(), calls=%async_computation.17 | async-start | bytes 2949120 | tf_op jit(solution)/shard_map/reduce_scatter | solution.py:296
  671.7 228.8 %reduce-scatter.10.cloned.1.call-start = ((), (), s32[]{:S(2)}) async-start(), calls=%async_computation.15 | async-start | bytes 2949120 | tf_op jit(solution)/shard_map/reduce_scatter | solution.py:294
  671.8 26.1 %copy-start.5 = (bf16[1024,768]{0,1:T(8,128)(2,1)S(1)}, bf16[1024,768]{0,1:T(8,128)(2,1)}, u32[]{:S(2)}) copy-start(bf16[1024,768]{0,1:T(8,128)(2,1)} %copy-done.4) | copy-start | bytes 4718596
  756.0 144.6 %reduce-scatter.12.cloned.1.call-start = ((), (), s32[]{:S(2)}) async-start(), calls=%async_computation.16 | async-start | bytes 2949120 | tf_op jit(solution)/shard_map/reduce_scatter | solution.py:295
  781.7 199.9 %all-gather.18.cloned.1.call-start = ((), (), s32[]{:S(2)}) async-start(), calls=%async_computation.22 | async-start | bytes 10616832 | tf_op jit(solution)/shard_map/all_gather | solution.py:322
  782.3 199.3 %all-gather.16.cloned.1.call-start = ((), (), s32[]{:S(2)}) async-start(), calls=%async_computation.20 | async-start | bytes 10616832 | tf_op jit(solution)/shard_map/all_gather | solution.py:321
  783.0 258.6 %all-reduce.11.cloned.1.call-start = ((), (), s32[]{:S(2)}) async-start(), calls=%async_computation.24 | async-start | bytes 4718592 | tf_op jit(solution)/shard_map/psum | solution.py:303
  816.4 31.0 %copy-start.17 = (bf16[1024,768]{0,1:T(8,128)(2,1)S(1)}, bf16[1024,768]{0,1:T(8,128)(2,1)}, u32[]{:S(2)}) copy-start(bf16[1024,768]{0,1:T(8,128)(2,1)} %get-tuple-element.80) | copy-start | bytes 4718596
  902.0 39.7 %copy-start.47 = (f32[768]{0:T(1024)S(1)}, f32[768]{0:T(1024)}, u32[]{:S(2)}) copy-start(f32[768]{0:T(1024)} %get-tuple-element.60) | copy-start | bytes 9220
  (50 other events, 274.1 us)
Sparse Core Ops, SparseCore 0:
  9.6 33.3 all-gather.9
  44.5 29.5 all-gather.11
  75.7 29.5 all-gather.7
  106.7 29.5 all-gather.13
  468.2 75.7 reduce-scatter.19
  547.9 76.4 reduce-scatter.17
  627.3 20.5 reduce-scatter.21
  650.3 46.2 reduce-scatter.15
  699.1 47.5 reduce-scatter.13
  756.1 47.1 reduce-scatter.9
  805.7 47.5 reduce-scatter.11
  855.2 58.3 all-gather.17
  915.6 58.7 all-gather.15
  978.2 63.3 all-reduce.10
where the time goes:
time: 1080 us; the launch traced here: 1070 us
  matrix products  387 us (36%)
  local copies, waits for them, and re-layouts  227 us (21%)
  blocking collectives  203 us (19%)
  other arithmetic  121 us (11%)
  waiting for transfers between devices  104 us (10%)
  between operations  17.2 us (2%)
    dot_general x2, matrix products, on_device(): jnp.einsum('vsi,dsi->dv', grad_scores, matches.astype(jnp.float32), preci...  77.7 us
    unnamed x159, local copies, waits for them, and re-layouts  73 us
    mul x2, local copies, waits for them, and re-layouts, on_device(): grad_scores = chances * (grad_chances - inner_sum)  62 us
    dot_general x2, local copies, waits for them, and re-layouts, block_scores(): jnp.einsum('rni,rf->fni', slot_indicators, relative_bias_table, preferred...  60.5 us
    psum x1, waiting for transfers between devices, on_device(): lax.psum((owned_grads[0], owned_grads[1], owned_grads[2], owned_grads[3],...  60 us
    mul x2, other arithmetic, on_device(): grad_scores = chances * (grad_chances - inner_sum)  52 us
    all_gather x1, blocking collectives, on_device(): lax.all_gather(w_router, 'shard', axis=0, tiled=True)  48.8 us
    all_to_all x1, blocking collectives, on_device(): lax.all_to_all(outgoing, 'shard', split_axis=0, concat_axis=1, tiled=True)  44.4 us
  transfers between devices with their start and end apart: 16, of which 2 were waited for; matrix products, arithmetic and copies ran while one was open for 58% of the time, Pallas kernels for 0%

commit v1 on v0

--- a/solution.py
+++ b/solution.py
@@ -167,7 +167,12 @@
     outgoing = jnp.einsum(
         "ect,td->ecd", places, normed_two, preferred_element_type=jnp.float32
     ).astype(jnp.bfloat16)
-    arrived = lax.all_to_all(outgoing, "shard", split_axis=0, concat_axis=1, tiled=True)
+    arrived = jnp.concatenate(
+        lax.all_to_all(
+            jnp.stack(jnp.split(outgoing, lax.axis_size("shard"), axis=0)), "shard", 0, 0
+        ),
+        axis=1,
+    )
     before_activation, hidden, result = expert_forward(
         arrived, expert_input_weight, expert_output_weight
     )

time: 1080 us -> 1090 us (level)
  no operation moved by 1% of the time
where the time goes in v1:
time: 1090 us; the launch traced here: 1080 us
  matrix products  386 us (35%)
  local copies, waits for them, and re-layouts  228 us (21%)
  blocking collectives  203 us (19%)
  other arithmetic  131 us (12%)
  waiting for transfers between devices  103 us (9%)
  between operations  17.2 us (2%)
    dot_general x2, matrix products, on_device(): jnp.einsum('vsi,dsi->dv', grad_scores, matches.astype(jnp.float32), preci...  77.7 us
    unnamed x159, local copies, waits for them, and re-layouts  73.2 us
    mul x2, local copies, waits for them, and re-layouts, on_device(): grad_scores = chances * (grad_chances - inner_sum)  62.1 us
    dot_general x2, local copies, waits for them, and re-layouts, block_scores(): jnp.einsum('rni,rf->fni', slot_indicators, relative_bias_table, preferred...  60.8 us
    psum x1, waiting for transfers between devices, on_device(): lax.psum((owned_grads[0], owned_grads[1], owned_grads[2], owned_grads[3],...  59.8 us
    mul x2, other arithmetic, on_device(): grad_scores = chances * (grad_chances - inner_sum)  52 us
    all_gather x1, blocking collectives, on_device(): lax.all_gather(w_router, 'shard', axis=0, tiled=True)  48.8 us
    all_to_all x1, blocking collectives, on_device(): lax.all_to_all(jnp.stack(jnp.split(outgoing, lax.axis_size('shard'), axis...  44.5 us
  transfers between devices with their start and end apart: 16, of which 2 were waited for; matrix products, arithmetic and copies ran while one was open for 58% of the time, Pallas kernels for 0%

profile of v1, /device:TPU:0, one launch (start us, length us, event | category | flops | bytes accessed | tf_op | source)
XLA Modules:
  0.0 1078.1 jit_solution(16910146176125769221)
XLA Ops:
  13.6 13.6 %all-reduce.8 = (bf16[768]{0:T(1024)(128)(2,1)S(1)}, bf16[768]{0:T(1024)(128)(2,1)S(1)}) all-reduce(bf16[768]{0:T(1024)(128)(2,1)S(1)} %dynamic-update-slice, bf16[768]{0:T(1024)(128)(2,1)S(1)} %dynamic-update-slice.1), channel_id=1, replica_groups=mesh['replica'=8,'shard'=4] {'shard'}, use_global_device_ids=true, to_apply=%add | all-reduce | flops 1536 | bytes 6144
  29.9 12.1 %all_gather.42 = bf16[32,12]{1,0:T(8,128)(2,1)S(1)} all-gather(bf16[8,12]{1,0:T(8,128)(2,1)} %param.25), channel_id=1, replica_groups=mesh['replica'=8,'shard'=4] {'shard'}, dimensions={0}, use_global_device_ids=true | all-gather | bytes 960 | tf_op jit(solution)/shard_map/all_gather | solution.py:88
  54.6 16.3 %fusion.1 = f32[512,1024,12]{0,2,1:T(8,128)} fusion(s32[512,1024]{0,1:T(8,128)S(1)} %fusion.85, bf16[32,12]{1,0:T(8,128)(2,1)S(1)} %all_gather.42), kind=kOutput, calls=%fused_computation.2 | convolution fusion | flops 419430400 | bytes 27263744 | tf_op jit(solution)/shard_map/rni,rf->fni/dot_general | solution.py:31
  70.9 30.2 %copy.81 = f32[512,1024,12]{1,0,2:T(8,128)} copy(f32[512,1024,12]{0,2,1:T(8,128)} %fusion.1) | data formatting | bytes 50331648 | tf_op jit(solution)/shard_map/rni,rf->fni/dot_general | solution.py:31
  101.1 16.6 %fusion.3 = f32[512,1024,12]{0,2,1:T(8,128)} fusion(s32[512,1024]{0,1:T(8,128)S(1)} %fusion.84, bf16[32,12]{1,0:T(8,128)(2,1)S(1)} %all_gather.42), kind=kOutput, calls=%fused_computation.5 | convolution fusion | flops 419430400 | bytes 27263744 | tf_op jit(solution)/shard_map/rni,rf->fni/dot_general | solution.py:31
  117.7 30.6 %copy.80 = f32[512,1024,12]{1,0,2:T(8,128)} copy(f32[512,1024,12]{0,2,1:T(8,128)} %fusion.3) | data formatting | bytes 50331648 | tf_op jit(solution)/shard_map/rni,rf->fni/dot_general | solution.py:31
  156.6 16.6 %fusion.161 = (f32[12,512]{1,0:T(8,128)S(1)}, f32[12,512,1024]{2,1,0:T(8,128)}) fusion(f32[512,1024,12]{1,0,2:T(8,128)} %copy.81, bf16[1024,12,64]{0,2,1:T(8,128)(2,1)S(1)} %bitcast.178, bf16[1,1024,12,64]{1,3,2,0:T(8,128)(2,1)} %bitcast.198, pred[512,1024]{1,0:T(8,128)(4,1)} %get-tuple-element.86), kind=kOutput, calls=%fused_computation.204 | convolution fusion | flops 824174592 | bytes 53239808 | tf_op jit(solution)/shard_map/qhe,khe->hqk/dot_general | solution.py:30
  173.2 20.4 %fusion.11 = f32[12,512]{1,0:T(8,128)S(1)} fusion(f32[12,512,1024]{2,1,0:T(8,128)} %get-tuple-element.92, f32[12,512]{1,0:T(8,128)S(1)} %get-tuple-element.91), kind=kLoop, calls=%fused_computation.27 | loop fusion | flops 12576768 | bytes 25214976 | tf_op jit(solution)/shard_map/reduce_sum | solution.py:141
  196.5 11.9 %fusion.133 = bf16[512,12,64]{0,2,1:T(8,128)(2,1)} fusion(bf16[1024,12,64]{0,2,1:T(8,128)(2,1)S(1)} %bitcast.188, f32[12,512,1024]{2,1,0:T(8,128)} %get-tuple-element.92, f32[12,512]{1,0:T(8,128)S(1)} %fusion.11, f32[12,512]{1,0:T(8,128)S(1)} %get-tuple-element.91), kind=kOutput, calls=%fused_computation.152 | convolution fusion | flops 824573952 | bytes 27574272 | tf_op jit(solution)/shard_map/hqk,khe->qhe/dot_general | solution.py:145
  208.5 15.7 %fusion.162 = (f32[12,512]{1,0:T(8,128)S(1)}, f32[12,512,1024]{2,1,0:T(8,128)}) fusion(f32[512,1024,12]{1,0,2:T(8,128)} %copy.80, bf16[1024,12,64]{0,2,1:T(8,128)(2,1)S(1)} %bitcast.179, bf16[1,1024,12,64]{1,3,2,0:T(8,128)(2,1)S(1)} %bitcast.199, pred[512,1024]{1,0:T(8,128)(4,1)} %get-tuple-element.85), kind=kOutput, calls=%fused_computation.205 | convolution fusion | flops 824174592 | bytes 53239808 | tf_op jit(solution)/shard_map/qhe,khe->hqk/dot_general | solution.py:30
  254.8 44.5 %all_to_all.38 = bf16[4,1,320,768]{3,2,1,0:T(8,128)(2,1)S(1)} all-to-all(bf16[4,1,320,768]{3,2,1,0:T(8,128)(2,1)S(1)} %pad_maximum_fusion), channel_id=1, replica_groups=mesh['replica'=8,'shard'=4] {'shard'}, dimensions={0} | all-to-all | bytes 3932160 | tf_op jit(solution)/shard_map/all_to_all | solution.py:171
  316.8 15.1 %copy.116 = bf16[1,1280,768]{2,0,1:T(2,128)(2,1)} copy(bf16[1,1280,768]{2,1,0:T(8,128)(2,1)S(1)} %fusion.70) | data formatting | bytes 3932160 | tf_op jit(solution)/shard_map/convert_element_type | solution.py:45
  332.3 13.7 %reduce.2 = bf16[1280,768]{1,0:T(8,128)(2,1)} reduce(bf16[1280,1,768]{2,1,0:T(2,128)(2,1)} %bitcast.182, bf16[]{:T(256)} %broadcast.378), dimensions={1}, to_apply=%bitcast.176.reduce_sub_computation | reduce | bytes 3932162
  354.5 48.8 %all-gather = bf16[4,192,4]{1,2,0:T(4,128)(2,1)S(1)} all-gather(bf16[1,192,4]{1,2,0:T(4,128)(2,1)S(1)} %bitcast.224), channel_id=1, replica_groups=mesh['replica'=8,'shard'=4] {'shard'}, dimensions={0}, use_global_device_ids=true | all-gather | bytes 7680 | tf_op jit(solution)/shard_map/all_gather | solution.py:87
  422.3 44.4 %all_to_all.39 = bf16[4,320,768]{2,1,0:T(8,128)(2,1)S(1)} all-to-all(bf16[4,320,768]{2,1,0:T(8,128)(2,1)S(1)} %fusion.107), channel_id=1, replica_groups=mesh['replica'=8,'shard'=4] {'shard'}, dimensions={0} | all-to-all | bytes 3932160 | tf_op jit(solution)/shard_map/all_to_all | solution.py:211
  478.1 18.7 %fusion.20 = bf16[1280,3072]{1,0:T(8,128)(2,1)S(1)} fusion(f32[1280,3072]{1,0:T(8,128)} %copy-done.54, bf16[1280,768]{1,0:T(8,128)(2,1)} %bitcast.205, bf16[1,3072,768]{2,1,0:T(8,128)(2,1)} %param.27), kind=kOutput, calls=%fused_computation.36 | convolution fusion | flops 6118440960 | bytes 30277632 | tf_op jit(solution)/shard_map/ecd,efd->ecf/dot_general | solution.py:50
  519.2 15.3 %copy.115 = bf16[1,1280,768]{2,0,1:T(2,128)(2,1)} copy(bf16[1,1280,768]{2,1,0:T(8,128)(2,1)S(1)} %fusion.73) | data formatting | bytes 3932160 | tf_op jit(solution)/shard_map/convert_element_type | solution.py:60
  534.5 13.8 %reduce.3 = bf16[1280,768]{1,0:T(8,128)(2,1)} reduce(bf16[1280,1,768]{2,1,0:T(2,128)(2,1)} %bitcast.183, bf16[]{:T(256)} %broadcast.378), dimensions={1}, to_apply=%bitcast.175.reduce_sub_computation | reduce | bytes 3932162
  560.4 39.6 %all-to-all-done.3 = bf16[4,2,122880]{2,1,0:T(2,128)(2,1)} async-done(((bf16[4,2,122880]{2,1,0:T(2,128)(2,1)}), bf16[4,2,122880]{2,1,0:T(2,128)(2,1)}, u32[]{:S(2)}, u32[]{:S(2)}) %all-to-all-start.3) | async-done | bytes 1966112 | tf_op jit(solution)/shard_map/all_to_all | solution.py:215
  649.2 16.2 %multiply_reduce_fusion = (f32[12,512]{1,0:T(8,128)S(1)}, f32[12,512,1024]{2,1,0:T(8,128)}) fusion(f32[12,512,1024]{2,1,0:T(8,128)} %get-tuple-element.92, f32[12,512]{1,0:T(8,128)S(1)} %log_add_fusion, bf16[1024,12,64]{0,2,1:T(8,128)(2,1)S(1)} %bitcast.190, bf16[1,1024,12,64]{1,3,2,0:T(8,128)(2,1)} %bitcast.196), kind=kOutput, calls=%fused_computation.15 | convolution fusion | flops 824174592 | bytes 52740096 | tf_op jit(solution)/shard_map/qhe,khe->hqk/dot_general | solution.py:256
  665.4 16.0 %multiply_reduce_fusion.1 = (f32[12,512]{1,0:T(8,128)S(1)}, f32[12,512,1024]{2,1,0:T(8,128)}) fusion(f32[12,512,1024]{2,1,0:T(8,128)} %get-tuple-element.94, f32[12,512]{1,0:T(8,128)S(1)} %log_add_fusion.1, bf16[1024,12,64]{0,2,1:T(8,128)(2,1)S(1)} %bitcast.191, bf16[1,1024,12,64]{1,3,2,0:T(8,128)(2,1)} %bitcast.197), kind=kOutput, calls=%fused_computation.18 | convolution fusion | flops 824174592 | bytes 52740096 | tf_op jit(solution)/shard_map/qhe,khe->hqk/dot_general | solution.py:256
  681.5 26.0 %subtract_multiply_fusion = f32[12,512,1024]{2,1,0:T(8,128)} fusion(f32[12,512,1024]{2,1,0:T(8,128)} %get-tuple-element.103, f32[12,512,1024]{2,1,0:T(8,128)} %get-tuple-element.92, f32[12,512]{1,0:T(8,128)S(1)} %get-tuple-element.102, f32[12,512]{1,0:T(8,128)S(1)} %log_add_fusion), kind=kLoop, calls=%fused_computation.14 | loop fusion | flops 18874368 | bytes 75546624 | tf_op jit(solution)/shard_map/mul | solution.py:260
  707.5 13.4 %fusion.126 = bf16[512,12,64]{0,2,1:T(8,128)(2,1)} fusion(bf16[1024,12,64]{0,2,1:T(8,128)(2,1)S(1)} %bitcast.180, f32[12,512,1024]{2,1,0:T(8,128)} %subtract_multiply_fusion), kind=kOutput, calls=%fused_computation.149 | convolution fusion | flops 811991040 | bytes 27525120 | tf_op jit(solution)/shard_map/hqk,khe->qhe/dot_general | solution.py:270
  720.9 26.0 %subtract_multiply_fusion.1 = f32[12,512,1024]{2,1,0:T(8,128)} fusion(f32[12,512,1024]{2,1,0:T(8,128)} %get-tuple-element.105, f32[12,512,1024]{2,1,0:T(8,128)} %get-tuple-element.94, f32[12,512]{1,0:T(8,128)S(1)} %get-tuple-element.104, f32[12,512]{1,0:T(8,128)S(1)} %log_add_fusion.1), kind=kLoop, calls=%fused_computation.17 | loop fusion | flops 18874368 | bytes 75546624 | tf_op jit(solution)/shard_map/mul | solution.py:260
  746.9 13.1 %fusion.129 = bf16[512,12,64]{0,2,1:T(8,128)(2,1)} fusion(bf16[1024,12,64]{0,2,1:T(8,128)(2,1)S(1)} %bitcast.181, f32[12,512,1024]{2,1,0:T(8,128)} %subtract_multiply_fusion.1), kind=kOutput, calls=%fused_computation.150 | convolution fusion | flops 811991040 | bytes 27525120 | tf_op jit(solution)/shard_map/hqk,khe->qhe/dot_general | solution.py:270
  795.0 31.1 %copy.94 = f32[12,512,1024]{1,0,2:T(8,128)} copy(f32[12,512,1024]{2,1,0:T(8,128)} %subtract_multiply_fusion) | data formatting | bytes 50331648 | tf_op jit(solution)/shard_map/mul | solution.py:260
  826.1 31.0 %copy.93 = f32[12,512,1024]{1,0,2:T(8,128)} copy(f32[12,512,1024]{2,1,0:T(8,128)} %subtract_multiply_fusion.1) | data formatting | bytes 50331648 | tf_op jit(solution)/shard_map/mul | solution.py:260
  872.1 38.0 %fusion.134 = f32[32,12]{1,0:T(8,128)S(1)} fusion(f32[12,512,1024]{1,0,2:T(8,128)} %copy.93, s32[512,1024]{0,1:T(8,128)S(1)} %copy-done.3), kind=kOutput, calls=%fused_computation.153 | convolution fusion | flops 2432696320 | bytes 27264512 | tf_op jit(solution)/shard_map/vsi,dsi->dv/dot_general | solution.py:261
  911.7 39.7 %fusion.136 = f32[32,12]{1,0:T(8,128)S(1)} fusion(f32[32,12]{1,0:T(8,128)S(1)} %fusion.134, f32[12,512,1024]{1,0,2:T(8,128)} %copy.94, s32[512,1024]{0,1:T(8,128)S(1)} %copy-done.1), kind=kOutput, calls=%fused_computation.155 | convolution fusion | flops 2432696832 | bytes 27266048 | tf_op jit(solution)/shard_map/vsi,dsi->dv/dot_general | solution.py:261
  951.5 17.3 %all-reduce.7 = (f32[768]{0:T(1024)S(1)}, f32[768]{0:T(1024)S(1)}, f32[32,12]{1,0:T(8,128)S(1)}) all-reduce(f32[768]{0:T(1024)S(1)} %get-tuple-element.62, f32[768]{0:T(1024)S(1)} %copy-done.47, f32[32,12]{1,0:T(8,128)S(1)} %fusion.136), channel_id=6, replica_groups=mesh['replica'=8,'shard'=4] {'shard'}, use_global_device_ids=true, to_apply=%region_26.27.clone | all-reduce | flops 1920 | bytes 15360
  968.9 22.7 %all-reduce.5 = (f32[192]{0:T(256)}, f32[192]{0:T(256)}, f32[192,4]{0,1:T(4,128)}, f32[8,12]{1,0:T(8,128)}) all-reduce(f32[192]{0:T(256)S(1)} %dynamic-slice.3, f32[192]{0:T(256)S(1)} %dynamic-slice.5, f32[192,4]{0,1:T(4,128)S(1)} %copy.108, ...), channel_id=1, replica_groups=mesh['replica'=8,'shard'=4] {'replica'}, use_global_device_ids=true, to_apply=%region_27.28 | all-reduce | flops 1248 | bytes 9984 | tf_op jit(solution)/shard_map/psum | solution.py:308
  991.7 59.8 %all-reduce.11.cloned.1.call-done = (f32[192,768]{1,0:T(8,128)}, f32[192,768]{1,0:T(8,128)}, f32[192,768]{1,0:T(8,128)}, f32[192,768]{1,0:T(8,128)}) async-done(((f32[192,768]{1,0:T(8,128)}, f32[192,768]{1,0:T(8,128)}, f32[192,768]{1,0:T(8,128)}, f32[192,768]{1,0:T(8,128)}), (f32[192,768]{1,0:T(8,128)}, f32[192,768]{1,0:T(8,128)}, f32[192,768]{1,0:T(8,128)}, ...) | async-done | bytes 2359312 | tf_op jit(solution)/shard_map/psum | solution.py:308
  (273 shorter events, 272.7 us)
Async XLA Ops:
  7.2 142.7 %all-gather.10.cloned.1.call-start = ((), (), s32[]{:S(2)}) async-start(), calls=%async_computation.12 | async-start | bytes 1474560 | tf_op jit(solution)/shard_map/all_gather | solution.py:81
  7.9 145.9 %all-gather.12.cloned.1.call-start = ((), (), s32[]{:S(2)}) async-start(), calls=%async_computation.13 | async-start | bytes 1474560 | tf_op jit(solution)/shard_map/all_gather | solution.py:82
  8.7 185.0 %all-gather.8.cloned.1.call-start = ((), (), s32[]{:S(2)}) async-start(), calls=%async_computation.11 | async-start | bytes 1474560 | tf_op jit(solution)/shard_map/all_gather | solution.py:83
  9.4 237.7 %all-gather.14.cloned.1.call-start = ((), (), s32[]{:S(2)}) async-start(), calls=%async_computation.14 | async-start | bytes 1474560 | tf_op jit(solution)/shard_map/all_gather | solution.py:84
  27.3 166.4 %copy-start.40 = (f32[768]{0:T(1024)}, f32[768]{0:T(1024)S(1)}, u32[]{:S(2)}) copy-start(f32[768]{0:T(1024)S(1)} %convert_element_type.284) | copy-start | bytes 9220
  49.1 144.6 %copy-start.42 = (f32[1024]{0:T(1024)}, f32[1024]{0:T(1024)S(1)}, u32[]{:S(2)}) copy-start(f32[1024]{0:T(1024)S(1)} %fusion.146) | copy-start | bytes 12292
  51.2 49.9 %copy-start.2 = (s32[512,1024]{0,1:T(8,128)}, s32[512,1024]{0,1:T(8,128)S(1)}, u32[]{:S(2)}) copy-start(s32[512,1024]{0,1:T(8,128)S(1)} %fusion.84) | copy-start | bytes 6291460
  117.7 30.6 %copy-start.46 = (s32[1,1024]{1,0:T(1,128)S(1)}, s32[1,1024]{1,0:T(1,128)}, u32[]{:S(2)}) copy-start(s32[1,1024]{1,0:T(1,128)} %param.16) | copy-start | bytes 12292
  117.7 32.3 %copy-start.7 = (bf16[1024,768]{0,1:T(8,128)(2,1)S(1)}, bf16[1024,768]{0,1:T(8,128)(2,1)}, u32[]{:S(2)}) copy-start(bf16[1024,768]{0,1:T(8,128)(2,1)} %copy-done.6) | copy-start | bytes 4718596
  156.6 51.8 %copy-start.4 = (bf16[1024,768]{0,1:T(8,128)(2,1)}, bf16[1024,768]{0,1:T(8,128)(2,1)S(1)}, u32[]{:S(2)}) copy-start(bf16[1024,768]{0,1:T(8,128)(2,1)S(1)} %convolution_convert_fusion.1) | copy-start | bytes 4718596
  247.1 53.5 %slice-start.5 = ((s8[4718592]{0:T(1024)(128)(4,1)}), s8[4194304]{0:T(1024)(128)(4,1)S(1)}, s32[]{:S(2)}) async-start(s8[4718592]{0:T(1024)(128)(4,1)} %bitcast.227), calls=%async_computation.30 | async-start | bytes 8388608
  251.7 48.9 %slice-start.6 = ((s8[4718592]{0:T(1024)(128)(4,1)}), s8[524288]{0:T(1024)(128)(4,1)S(1)}, s32[]{:S(2)}) async-start(s8[4718592]{0:T(1024)(128)(4,1)} %bitcast.227), calls=%async_computation.31 | async-start | bytes 1048576
  254.5 52.5 %slice-start.3 = ((s8[4718592]{0:T(1024)(128)(4,1)}), s8[4194304]{0:T(1024)(128)(4,1)S(1)}, s32[]{:S(2)}) async-start(s8[4718592]{0:T(1024)(128)(4,1)} %bitcast.225), calls=%async_computation.28 | async-start | bytes 8388608
  350.0 58.1 %all-to-all-start.1 = ((bf16[4,2,122880]{2,1,0:T(2,128)(2,1)}), bf16[4,2,122880]{2,1,0:T(2,128)(2,1)}, u32[]{:S(2)}, u32[]{:S(2)}) async-start(bf16[4,2,122880]{2,1,0:T(2,128)(2,1)} %reshape.406), calls=%async_computation.1 | async-start | bytes 3932160 | tf_op jit(solution)/shard_map/all_to_all | solution.py:179
  354.4 437.0 %reduce-scatter.20.cloned.1.call-start = ((), (), s32[]{:S(2)}) async-start(), calls=%async_computation.21 | async-start | bytes 10616832 | tf_op jit(solution)/shard_map/reduce_scatter | solution.py:323
  415.5 52.5 %slice-start.7 = ((s8[15728640]{0:T(1024)(128)(4,1)}), s8[4194304]{0:T(1024)(128)(4,1)S(1)}, s32[]{:S(2)}) async-start(s8[15728640]{0:T(1024)(128)(4,1)} %bitcast.229), calls=%async_computation.32 | async-start | bytes 8388608
  415.5 52.5 %slice-start.8 = ((s8[15728640]{0:T(1024)(128)(4,1)}), s8[4194304]{0:T(1024)(128)(4,1)S(1)}, s32[]{:S(2)}) async-start(s8[15728640]{0:T(1024)(128)(4,1)} %bitcast.229), calls=%async_computation.33 | async-start | bytes 8388608
  419.6 48.4 %slice-start.9 = ((s8[15728640]{0:T(1024)(128)(4,1)}), s8[4194304]{0:T(1024)(128)(4,1)S(1)}, s32[]{:S(2)}) async-start(s8[15728640]{0:T(1024)(128)(4,1)} %bitcast.229), calls=%async_computation.34 | async-start | bytes 8388608
  419.6 48.4 %slice-start.10 = ((s8[15728640]{0:T(1024)(128)(4,1)}), s8[3145728]{0:T(1024)(128)(4,1)S(1)}, s32[]{:S(2)}) async-start(s8[15728640]{0:T(1024)(128)(4,1)} %bitcast.229), calls=%async_computation.35 | async-start | bytes 6291456
  478.0 313.9 %reduce-scatter.18.cloned.1.call-start = ((), (), s32[]{:S(2)}) async-start(), calls=%async_computation.19 | async-start | bytes 10616832 | tf_op jit(solution)/shard_map/reduce_scatter | solution.py:322
  552.2 47.7 %all-to-all-start.3 = ((bf16[4,2,122880]{2,1,0:T(2,128)(2,1)}), bf16[4,2,122880]{2,1,0:T(2,128)(2,1)}, u32[]{:S(2)}, u32[]{:S(2)}) async-start(bf16[4,2,122880]{2,1,0:T(2,128)(2,1)} %reshape.408), calls=%async_computation.3 | async-start | bytes 3932160 | tf_op jit(solution)/shard_map/all_to_all | solution.py:215
  556.6 237.4 %reduce-scatter.22.cloned.1.call-start = ((), (), s32[]{:S(2)}) async-start(), calls=%async_computation.23 | async-start | bytes 491520
  560.3 349.8 %reduce-scatter.16.cloned.1.call-start = ((), (), s32[]{:S(2)}) async-start(), calls=%async_computation.18 | async-start | bytes 2949120 | tf_op jit(solution)/shard_map/reduce_scatter | solution.py:302
  619.9 290.3 %reduce-scatter.14.cloned.1.call-start = ((), (), s32[]{:S(2)}) async-start(), calls=%async_computation.17 | async-start | bytes 2949120 | tf_op jit(solution)/shard_map/reduce_scatter | solution.py:301
  681.4 228.8 %reduce-scatter.10.cloned.1.call-start = ((), (), s32[]{:S(2)}) async-start(), calls=%async_computation.15 | async-start | bytes 2949120 | tf_op jit(solution)/shard_map/reduce_scatter | solution.py:299
  681.5 26.0 %copy-start.5 = (bf16[1024,768]{0,1:T(8,128)(2,1)S(1)}, bf16[1024,768]{0,1:T(8,128)(2,1)}, u32[]{:S(2)}) copy-start(bf16[1024,768]{0,1:T(8,128)(2,1)} %copy-done.4) | copy-start | bytes 4718596
  765.6 144.7 %reduce-scatter.12.cloned.1.call-start = ((), (), s32[]{:S(2)}) async-start(), calls=%async_computation.16 | async-start | bytes 2949120 | tf_op jit(solution)/shard_map/reduce_scatter | solution.py:300
  791.3 200.3 %all-gather.18.cloned.1.call-start = ((), (), s32[]{:S(2)}) async-start(), calls=%async_computation.22 | async-start | bytes 10616832 | tf_op jit(solution)/shard_map/all_gather | solution.py:327
  791.9 199.8 %all-gather.16.cloned.1.call-start = ((), (), s32[]{:S(2)}) async-start(), calls=%async_computation.20 | async-start | bytes 10616832 | tf_op jit(solution)/shard_map/all_gather | solution.py:326
  792.6 258.8 %all-reduce.11.cloned.1.call-start = ((), (), s32[]{:S(2)}) async-start(), calls=%async_computation.24 | async-start | bytes 4718592 | tf_op jit(solution)/shard_map/psum | solution.py:308
  826.1 31.0 %copy-start.17 = (bf16[1024,768]{0,1:T(8,128)(2,1)S(1)}, bf16[1024,768]{0,1:T(8,128)(2,1)}, u32[]{:S(2)}) copy-start(bf16[1024,768]{0,1:T(8,128)(2,1)} %get-tuple-element.80) | copy-start | bytes 4718596
  911.7 39.7 %copy-start.47 = (f32[768]{0:T(1024)S(1)}, f32[768]{0:T(1024)}, u32[]{:S(2)}) copy-start(f32[768]{0:T(1024)} %get-tuple-element.60) | copy-start | bytes 9220
  (50 other events, 282.9 us)
Sparse Core Ops, SparseCore 0:
  9.6 33.3 all-gather.9
  44.5 29.5 all-gather.11
  75.7 29.5 all-gather.7
  106.7 29.5 all-gather.13
  478.2 75.7 reduce-scatter.19
  557.9 76.4 reduce-scatter.17
  637.2 20.5 reduce-scatter.21
  660.3 46.3 reduce-scatter.15
  709.0 47.5 reduce-scatter.13
  765.7 47.3 reduce-scatter.9
  815.5 47.5 reduce-scatter.11
  865.0 58.3 all-gather.17
  925.4 58.7 all-gather.15
  988.0 63.4 all-reduce.10
